TPU v7x, 128 devices: a whole 4x4x4 slice. The times are simulated.
128 devices in a mesh: seq: 32 (over x_lo, z, y), kvh: 4 (over x_hi, core).
Axes of the slice: x: 4 (x_hi: 2, x_lo: 2; x = x_hi * 2 + x_lo), y: 4, z: 4, core: 2. Of those that a mesh axis runs over, the one named last changes fastest.
Arguments:
- queries: bfloat16 [32, 3584], P('seq', 'kvh'), may hold values from -120 to 120
- keys: bfloat16 [2048, 512, 512], P('seq', None, 'kvh'), may hold values from -6 to 6
- values: bfloat16 [2048, 512, 512], P('seq', None, 'kvh'), may hold values from -24 to 24
- new_keys: bfloat16 [8, 4, 512], P(None, None, 'kvh'), may hold values from -6 to 6
- new_values: bfloat16 [8, 4, 512], P(None, None, 'kvh'), may hold values from -24 to 24
- cache_len: int32 [8], replicated, may hold values from 65025 to 393216, as said below
- block_request: int32 [2048], P('seq'), may hold values from 0 to 7, as said below
- block_index: int32 [2048], P('seq'), may hold values from 0 to 767, as said below
Outputs:
- attended: bfloat16 [32, 3584], P('seq', 'kvh')
Inputs may be any that keep to these rules, and one draw needn't show every extreme that they name: `cache_len`: exactly one request has 768 blocks and length 393216; every other request has at least 128 blocks, and its length lies in its last block. `block_request`: request r holds ceil(cache_len[r] / 512) blocks in all, spread over the devices. The blocks of request r carry block_index 0 to ceil(cache_len[r] / 512) - 1, each once.
All inputs are finite; a program needn't handle non-finite values.
Results may differ from a plain program's by a relative error of at most 0.0028.
Values may be sent and summed in bfloat16 or wider, within the bound.
A program may use at most 64 MiB of HBM per device.

v0:
```python
import math

import jax
import jax.numpy as jnp
from jax import lax
from jax.experimental import pallas as pl
from jax.experimental.pallas import tpu as pltpu
from jax.sharding import PartitionSpec as P

R = 8
STEPS = 4
HD = 128
GROUP = 7
ROWS = 32
BLOCK = 512
NBLK = 64
COUNT = 32
LAG = 8
CHUNK = 16
NCHUNK = NBLK // CHUNK
FLOOR = -1e30
RATE = math.log2(math.e) / math.sqrt(HD)
MESH = pl.DeviceIdType.MESH


def hops(k):
    ring = (0, 1, 2, 1)
    return k // 16 + ring[k // 4 % 4] + ring[k % 4]


PEERS = sorted(range(1, COUNT), key=hops, reverse=True)


def kernel(
    q_hbm, k_hbm, v_hbm, nk_hbm, nv_hbm, len_hbm, req_hbm, idx_hbm, out_ref,
    kb, vb, kt, wb, keep, sm, sl, sa, qrow, qbuf, qs, nk, nv, msg, part,
    clen, req, idx, prev, ksem, vsem, small, q_send, q_recv, p_send, p_recv,
):
    me = lax.axis_index("seq")

    barrier = pltpu.get_barrier_semaphore()
    for k in PEERS:
        pl.semaphore_signal(barrier, inc=1, device_id={"seq": me ^ k}, device_id_type=MESH)

    small_copies = [
        pltpu.make_async_copy(src, dst, small.at[i])
        for i, (src, dst) in enumerate(
            ((q_hbm, qrow), (req_hbm, req), (idx_hbm, idx), (len_hbm, clen), (nk_hbm, nk), (nv_hbm, nv))
        )
    ]
    for copy in small_copies:
        copy.start()

    def k_copy(i):
        rows = pl.ds(i * CHUNK, CHUNK)
        return pltpu.make_async_copy(k_hbm.at[rows], kb.at[rows], ksem.at[i])

    def v_copy(i):
        rows = pl.ds(i * CHUNK, CHUNK)
        return pltpu.make_async_copy(v_hbm.at[rows], vb.at[rows], vsem.at[i])

    for i in range(NCHUNK):
        k_copy(i).start()
    for i in range(NCHUNK):
        v_copy(i).start()

    small_copies[0].wait()
    own = qrow[...].astype(jnp.float32)
    own = jnp.concatenate(
        [own[:, g * HD : (g + 1) * HD] for g in range(GROUP)] + [jnp.zeros((1, HD), jnp.float32)],
        axis=0,
    )
    qbuf[me] = own.astype(jnp.bfloat16)
    pl.semaphore_wait(barrier, COUNT - 1)
    for k in PEERS:
        pltpu.make_async_remote_copy(
            src_ref=qbuf.at[me],
            dst_ref=qbuf.at[me],
            send_sem=q_send,
            recv_sem=q_recv,
            device_id={"seq": me ^ k},
            device_id_type=MESH,
        ).start()

    for copy in small_copies[1:]:
        copy.wait()
    sm[0] = jnp.full((ROWS, HD), FLOOR, jnp.float32)
    sl[0] = jnp.zeros((ROWS, HD), jnp.float32)
    sa[0] = jnp.zeros((ROWS, HD), jnp.float32)

    def link(b, last):
        r = req[b]
        before = last[0]
        for j in range(1, R):
            before = jnp.where(r == j, last[j], before)
        prev[b] = before
        return tuple(jnp.where(r == j, b + 1, last[j]) for j in range(R))

    last = lax.fori_loop(0, NBLK, link, tuple(jnp.int32(0) for _ in range(R)))

    lane8 = lax.broadcasted_iota(jnp.int32, (8, HD), 1)
    row8 = lax.broadcasted_iota(jnp.int32, (8, HD), 0)

    own_request = me // STEPS
    own_step = me % STEPS
    fresh_k = nk[own_request].astype(jnp.float32)
    fresh_v = nv[own_request].astype(jnp.float32)
    fresh_s = []
    for u in range(STEPS):
        s = jnp.sum(own * fresh_k[u : u + 1, :], axis=1, keepdims=True)
        fresh_s.append(jnp.where(u <= own_step, jnp.broadcast_to(s, (8, HD)), FLOOR))
    fresh_m = fresh_s[0]
    for u in range(1, STEPS):
        fresh_m = jnp.maximum(fresh_m, fresh_s[u])
    fresh_l = jnp.zeros((8, HD), jnp.float32)
    fresh_a = jnp.zeros((8, HD), jnp.float32)
    for u in range(STEPS):
        w = jnp.exp2((fresh_s[u] - fresh_m) * RATE).astype(jnp.bfloat16).astype(jnp.float32)
        fresh_l = fresh_l + w
        fresh_a = fresh_a + w * fresh_v[u : u + 1, :]

    def turn(*columns):
        picked = 0.0
        for i, column in enumerate(columns):
            picked = jnp.where(lane8 == row8 + 8 * i, column, picked)
        return jnp.sum(picked, axis=0, keepdims=True)

    fresh_m_row = turn(fresh_m)
    fresh_l_row = turn(fresh_l)

    def turn_keys(i, _):
        for u in range(4):
            kt[i * 4 + u] = kb[i * 4 + u].T
        return 0

    for i in range(NCHUNK):
        k_copy(i).wait()
        lax.fori_loop(i * CHUNK // 4, (i + 1) * CHUNK // 4, turn_keys, 0)

    for i in range(NCHUNK):
        v_copy(i).wait()

    others = qbuf.at[pl.ds(0, COUNT - 1)]
    pltpu.make_async_copy(others, others, q_recv).wait()
    for r in range(R):
        qs[r] = qbuf[r * STEPS : (r + 1) * STEPS].astype(jnp.float32).reshape(ROWS, HD).astype(jnp.bfloat16)

    lane = lax.broadcasted_iota(jnp.int32, (ROWS, HD), 1)

    def weigh(b):
        s = jnp.dot(qs[req[b]], kt[b], preferred_element_type=jnp.float32)
        limit = clen[req[b]] - idx[b] * BLOCK
        scores = []
        most = None
        for t in range(0, BLOCK, HD):
            x = jnp.where(lane < limit - t, s[:, t : t + HD], FLOOR)
            scores.append(x)
            most = x if most is None else jnp.maximum(most, x)
        before = sm[prev[b]]
        best = jnp.maximum(before, jnp.broadcast_to(jnp.max(most, axis=1, keepdims=True), (ROWS, HD)))
        sm[b + 1] = best
        shrink = jnp.exp2((before - best) * RATE)
        keep[b] = shrink
        total = None
        for t, x in zip(range(0, BLOCK, HD), scores):
            w = jnp.exp2((x - best) * RATE)
            total = w if total is None else total + w
            wb[b, :, t : t + HD] = w.astype(jnp.bfloat16)
        sl[b + 1] = sl[prev[b]] * shrink + total

    def gather_values(b):
        o = jnp.dot(wb[b], vb[b], preferred_element_type=jnp.float32)
        sa[b + 1] = sa[prev[b]] * keep[b] + o

    for b in range(NBLK + LAG):
        if b < NBLK:
            weigh(b)
        if b >= LAG:
            gather_values(b - LAG)

    for r in range(R):
        m = sm[last[r]]
        l = jnp.broadcast_to(jnp.sum(sl[last[r]], axis=1, keepdims=True), (ROWS, HD))
        for s in range(STEPS):
            rows = slice(s * 8, s * 8 + 8)
            msg[r * STEPS + s] = jnp.broadcast_to(turn(m[rows], l[rows]), (8, HD))

    for r in range(R):
        a = sa[last[r]]
        for s in range(STEPS):
            d = r * STEPS + s
            msg[d] = jnp.where(row8 == 7, msg[d], a[s * 8 : s * 8 + 8])
    for k in PEERS:
        pltpu.make_async_remote_copy(
            src_ref=msg.at[me ^ k],
            dst_ref=part.at[me],
            send_sem=p_send,
            recv_sem=p_recv,
            device_id={"seq": me ^ k},
            device_id_type=MESH,
        ).start()
    part[me] = msg[me]
    others = part.at[pl.ds(0, COUNT - 1)]
    pltpu.make_async_copy(others, others, p_recv).wait()

    m = part[:, 7, :]
    l = pltpu.roll(m, HD - 8, 1)
    best = jnp.maximum(jnp.max(m, axis=0, keepdims=True), fresh_m_row)
    w = jnp.exp2((m - best) * RATE)
    fresh_w = jnp.exp2((fresh_m_row - best) * RATE)
    total = jnp.sum(w * l, axis=0, keepdims=True) + fresh_w * fresh_l_row
    w = w / total
    fresh_w = fresh_w / total

    def spread(row):
        picked = jnp.where(lane8 == row8, jnp.broadcast_to(row, (8, HD)), 0.0)
        return jnp.sum(picked, axis=1, keepdims=True)

    out = spread(fresh_w) * fresh_a
    for i in range(COUNT):
        out = out + spread(w[i : i + 1, :]) * part[i]
    out_ref[...] = jnp.concatenate([out[g : g + 1, :] for g in range(GROUP)], axis=1).astype(jnp.bfloat16)

    sent = qbuf.at[pl.ds(0, COUNT - 1)]
    pltpu.make_async_copy(sent, sent, q_send).wait()
    sent = msg.at[pl.ds(0, COUNT - 1)]
    pltpu.make_async_copy(sent, sent, p_send).wait()


def shards(queries, keys, values, new_keys, new_values, cache_len, block_request, block_index):
    f32, bf16, i32 = jnp.float32, jnp.bfloat16, jnp.int32
    dma = pltpu.SemaphoreType.DMA
    return pl.pallas_call(
        kernel,
        out_shape=pltpu.VMEM((1, GROUP * HD), bf16),
        in_specs=[pl.BlockSpec(memory_space=pltpu.HBM)] * 8,
        out_specs=pl.BlockSpec(memory_space=pltpu.VMEM),
        scratch_shapes=[
            pltpu.VMEM((NBLK, BLOCK, HD), bf16),
            pltpu.VMEM((NBLK, BLOCK, HD), bf16),
            pltpu.VMEM((NBLK, HD, BLOCK), bf16),
            pltpu.VMEM((NBLK, ROWS, BLOCK), bf16),
            pltpu.VMEM((NBLK, ROWS, HD), f32),
            pltpu.VMEM((NBLK + 1, ROWS, HD), f32),
            pltpu.VMEM((NBLK + 1, ROWS, HD), f32),
            pltpu.VMEM((NBLK + 1, ROWS, HD), f32),
            pltpu.VMEM((1, GROUP * HD), bf16),
            pltpu.VMEM((COUNT, 8, HD), bf16),
            pltpu.VMEM((R, ROWS, HD), bf16),
            pltpu.VMEM((R, STEPS, HD), bf16),
            pltpu.VMEM((R, STEPS, HD), bf16),
            pltpu.VMEM((COUNT, 8, HD), f32),
            pltpu.VMEM((COUNT, 8, HD), f32),
            pltpu.SMEM((R,), i32),
            pltpu.SMEM((NBLK,), i32),
            pltpu.SMEM((NBLK,), i32),
            pltpu.SMEM((NBLK,), i32),
            dma((NCHUNK,)),
            dma((NCHUNK,)),
            dma((6,)),
            dma,
            dma,
            dma,
            dma,
        ],
        compiler_params=pltpu.CompilerParams(
            collective_id=0, has_side_effects=True, vmem_limit_bytes=63 * 2**20
        ),
        name="attend",
    )(queries, keys, values, new_keys, new_values, cache_len, block_request, block_index)


def solution(mesh):
    return jax.shard_map(
        shards,
        mesh=mesh,
        in_specs=(
            P("seq", "kvh"),
            P("seq", None, "kvh"),
            P("seq", None, "kvh"),
            P(None, None, "kvh"),
            P(None, None, "kvh"),
            P(),
            P("seq"),
            P("seq"),
        ),
        out_specs=P("seq", "kvh"),
        check_vma=False,
    )
```

profile of v0, /device:TPU:0, one launch (start us, length us, event | category | flops | bytes accessed | tf_op | source)
XLA Modules:
  0.0 21.6 jit_solution(14983761211630468298)
XLA Ops:
  0.0 21.0 %attend.1 = bf16[1,896]{1,0:T(2,128)(2,1)S(1)} custom-call(bf16[1,896]{1,0:T(2,128)(2,1)} %q_hbm.1, bf16[64,512,128]{2,1,0:T(8,128)(2,1)} %k_hbm.1, bf16[64,512,128]{2,1,0:T(8,128)(2,1)} %v_hbm.1, bf16[8,4,128]{2,1,0:T(4,128)(2,1)} %nk_hbm.1, bf16[8,4,128]{2,1,0:T(4,128)(2,1)} %nv_hbm.1, s32[8]{0:T(128)} %len_hbm.1, s32[64]{0:T(128)} %req_hbm.1, s32[64]{0:T(128)} %idx_hbm.1), custom_call_target="tpu_custom_call" | custom-call | tf_op jit(solution)/shard_map/attend/pallas_call | solution.py:233
  21.0 0.6 %copy.10 = bf16[1,896]{1,0:T(2,128)(2,1)} copy(bf16[1,896]{1,0:T(2,128)(2,1)S(1)} %attend.1) | data formatting | bytes 3584
where the time goes:
time: 21.7 us; the launch traced here: 21.6 us
  Pallas kernels  21 us (97%)
  local copies, waits for them, and re-layouts  0.58 us (3%)
    pallas_call x1, Pallas kernels, shards(): pl.pallas_call(kernel, out_shape=pltpu.VMEM((1, GROUP * HD), bf16), in_sp...  21 us
    unnamed x1, local copies, waits for them, and re-layouts  0.58 us

commit v1 on v0

--- a/solution.py
+++ b/solution.py
@@ -28,6 +28,10 @@
     return k // 16 + ring[k // 4 % 4] + ring[k % 4]
 
 
+def peer(me, k):
+    return (me // 16 + k // 16) % 2 * 16 + (me // 4 + k // 4) % 4 * 4 + (me + k) % 4
+
+
 PEERS = sorted(range(1, COUNT), key=hops, reverse=True)
 
 
@@ -40,7 +44,7 @@
 
     barrier = pltpu.get_barrier_semaphore()
     for k in PEERS:
-        pl.semaphore_signal(barrier, inc=1, device_id={"seq": me ^ k}, device_id_type=MESH)
+        pl.semaphore_signal(barrier, inc=1, device_id={"seq": peer(me, k)}, device_id_type=MESH)
 
     small_copies = [
         pltpu.make_async_copy(src, dst, small.at[i])
@@ -78,7 +82,7 @@
             dst_ref=qbuf.at[me],
             send_sem=q_send,
             recv_sem=q_recv,
-            device_id={"seq": me ^ k},
+            device_id={"seq": peer(me, k)},
             device_id_type=MESH,
         ).start()
 
@@ -192,11 +196,11 @@
             msg[d] = jnp.where(row8 == 7, msg[d], a[s * 8 : s * 8 + 8])
     for k in PEERS:
         pltpu.make_async_remote_copy(
-            src_ref=msg.at[me ^ k],
+            src_ref=msg.at[peer(me, k)],
             dst_ref=part.at[me],
             send_sem=p_send,
             recv_sem=p_recv,
-            device_id={"seq": me ^ k},
+            device_id={"seq": peer(me, k)},
             device_id_type=MESH,
         ).start()
     part[me] = msg[me]

time: 21.7 us -> 21.5 us (level)
  no operation moved by 1% of the time
where the time goes in v1:
time: 21.5 us; the launch traced here: 21.4 us
  Pallas kernels  20.8 us (97%)
  local copies, waits for them, and re-layouts  0.58 us (3%)
    pallas_call x1, Pallas kernels, shards(): pl.pallas_call(kernel, out_shape=pltpu.VMEM((1, GROUP * HD), bf16), in_sp...  20.8 us
    unnamed x1, local copies, waits for them, and re-layouts  0.58 us

profile of v1, /device:TPU:0, one launch (start us, length us, event | category | flops | bytes accessed | tf_op | source)
XLA Modules:
  0.0 21.4 jit_solution(10695199735744830944)
XLA Ops:
  0.0 20.8 %attend.1 = bf16[1,896]{1,0:T(2,128)(2,1)S(1)} custom-call(bf16[1,896]{1,0:T(2,128)(2,1)} %q_hbm.1, bf16[64,512,128]{2,1,0:T(8,128)(2,1)} %k_hbm.1, bf16[64,512,128]{2,1,0:T(8,128)(2,1)} %v_hbm.1, bf16[8,4,128]{2,1,0:T(4,128)(2,1)} %nk_hbm.1, bf16[8,4,128]{2,1,0:T(4,128)(2,1)} %nv_hbm.1, s32[8]{0:T(128)} %len_hbm.1, s32[64]{0:T(128)} %req_hbm.1, s32[64]{0:T(128)} %idx_hbm.1), custom_call_target="tpu_custom_call" | custom-call | tf_op jit(solution)/shard_map/attend/pallas_call | solution.py:237
  20.9 0.6 %copy.10 = bf16[1,896]{1,0:T(2,128)(2,1)} copy(bf16[1,896]{1,0:T(2,128)(2,1)S(1)} %attend.1) | data formatting | bytes 3584
